TPU v7x, 32 devices: a whole 2x2x4 slice. The times are simulated.
32 devices in a mesh: dp: 4 (over x, core), col: 8 (over z, y).
Axes of the slice: x: 2, y: 2, z: 4, core: 2. Of those that a mesh axis runs over, the one named last changes fastest.
Arguments:
- inputs: bfloat16 [32, 1024, 1024], P('dp', 'col'), may hold values from -6 to 6
- starts: int32 [32, 1024], P('dp', 'col'), may hold values from 0 to 1023, as said below
- cotangent: bfloat16 [32, 1024, 1024], P('dp', 'col'), may hold values from -6 to 6
- first_norm_gain: bfloat16 [1024], replicated, may hold values from 0.5 to 1.5
- shift_one: bfloat16 [1024], replicated, may hold values from -1.75 to 1.75
- w_qkv: bfloat16 [1024, 3072], replicated, may hold values from -0.1875 to 0.1875
- b_qkv: bfloat16 [3072], replicated, may hold values from -1.75 to 1.75
- w_out: bfloat16 [1024, 1024], replicated, may hold values from -1 to 1
- b_out: bfloat16 [1024], replicated, may hold values from -1.75 to 1.75
- second_norm_gain: bfloat16 [1024], replicated, may hold values from 0.5 to 1.5
- shift_two: bfloat16 [1024], replicated, may hold values from -1.75 to 1.75
- w_fc: bfloat16 [1024, 4096], replicated, may hold values from -0.1875 to 0.1875
- b_fc: bfloat16 [4096], replicated, may hold values from -1.75 to 1.75
- w_proj: bfloat16 [4096, 1024], replicated, may hold values from -0.09375 to 0.09375
- b_proj: bfloat16 [1024], replicated, may hold values from -1.75 to 1.75
- prefix_table: float32 [10, 512], replicated, may hold values from -6 to 6
- rep_w1: float32 [512, 512], replicated, may hold values from -0.25 to 0.25
- rep_b1: float32 [512], replicated, may hold values from -3 to 3
- rep_w2: float32 [512, 2048], P(None, 'col'), may hold values from -0.25 to 0.25
- rep_b2: float32 [2048], P('col'), may hold values from -3 to 3
Outputs:
- output: bfloat16 [32, 1024, 1024], P('dp', 'col')
- grad_input: bfloat16 [32, 1024, 1024], P('dp', 'col')
- grad_table: float32 [10, 512], replicated
- grad_w1: float32 [512, 512], replicated
- grad_b1: float32 [512], replicated
- grad_w2: float32 [512, 2048], P(None, 'col')
- grad_b2: float32 [2048], P('col')
Inputs may be any that keep to these rules, and one draw needn't show every extreme that they name: starts[r, q] is the first position of the document that holds token q of packed row r: it is equal over a document, equals q at a document's first token; position 0 begins a document, and position 1023 begins a document of one token in every packed row.
All inputs are finite; a program needn't handle non-finite values.
Results may differ from a plain program's by a relative error of at most 0.013.
Values may be sent and summed in bfloat16 or wider, within the bound.
A program may use at most 512 MiB of HBM per device.

v0:
```python
import functools

import jax
import jax.numpy as jnp
from jax import lax
from jax.experimental import pallas as pl
from jax.experimental.pallas import tpu as pltpu
from jax.sharding import PartitionSpec as P

H = 16
HEAD = 64
PAIR = 2 * HEAD
BLOCK = 256
PRE = 16
VMEM_BYTES = 62 << 20

epsilon = 1e-05
gelu_coef = 0.7978845608028654
cubic_coef = 0.044715
low_type = jnp.bfloat16
wide = jnp.float32
NT = (((1,), (1,)), ((), ()))
TN = (((0,), (0,)), ((), ()))
MESH = pl.DeviceIdType.MESH
ANY = pl.BlockSpec(memory_space=pl.ANY)
VM = pl.BlockSpec(memory_space=pltpu.VMEM)


def standardize(values):
    center = values - jnp.mean(values, axis=-1, keepdims=True)
    inverse = lax.rsqrt(jnp.mean(center * center, axis=-1, keepdims=True) + epsilon)
    return center * inverse, inverse


def norm_backward_pass(gradient, norm_gain, normed, inverse):
    scaled = gradient * norm_gain
    centered = scaled - jnp.mean(scaled, axis=-1, keepdims=True)
    return inverse * (centered - normed * jnp.mean(scaled * normed, axis=-1, keepdims=True))


def gelu_parts(upper):
    square = upper * upper
    tangent = jnp.tanh(upper * (gelu_coef + (gelu_coef * cubic_coef) * square))
    half = 0.5 * upper
    share = 0.5 + 0.5 * tangent
    slope = share + half * (1.0 - tangent * tangent) * (
        gelu_coef + (3.0 * gelu_coef * cubic_coef) * square
    )
    return upper * share, slope


def dot_nt(a, b):
    return lax.dot_general(a, b, NT, preferred_element_type=wide)


def dot(a, b):
    return jnp.dot(a, b, preferred_element_type=wide)


def head_mask(values, which):
    lane = lax.broadcasted_iota(jnp.int32, values.shape, 1)
    keep = (lane < HEAD) if which == 0 else (lane >= HEAD)
    return jnp.where(keep, values, jnp.zeros_like(values))


def token_mask(scores, start, block_q, block_k):
    key = block_k * BLOCK + lax.broadcasted_iota(jnp.int32, scores.shape, 0)
    keep = key >= start
    if block_q == block_k:
        query = block_q * BLOCK + lax.broadcasted_iota(jnp.int32, scores.shape, 1)
        keep = keep & (key <= query)
    return jnp.where(keep, scores, -jnp.inf)


def prefix_mask(scores, count):
    key = lax.broadcasted_iota(jnp.int32, scores.shape, 0)
    return jnp.where(key < count, scores, -jnp.inf)


def masked(scores, count, start, block_q, block_k):
    if block_k < 0:
        return prefix_mask(scores, count)
    return token_mask(scores, start, block_q, block_k)


def key_chunks(block_q):
    tokens = [(c, PRE + c * BLOCK, PRE + (c + 1) * BLOCK) for c in range(block_q + 1)]
    return [(-1, 0, PRE)] + tokens


def transposed(values):
    return values.astype(wide).T.astype(low_type)


def attention_forward_pair(count, blocks, starts, q, k, v, pk, pv, out, lse, ke, vt, s_all, p_all, o_two):
    ke[0:PRE, :] = pk[...]
    ke[PRE:, :] = k[...]
    vt[:, 0:PRE] = transposed(pv[...])
    vt[:, PRE:] = transposed(v[...])
    units = [(i, h) for i in range(blocks) for h in range(2)]

    def view(u):
        return slice((u % 2) * BLOCK, (u % 2 + 1) * BLOCK)

    def score(u):
        i, h = units[u]
        rows = slice(i * BLOCK, (i + 1) * BLOCK)
        mine = head_mask(q[rows, :], h)
        start = starts[:, rows]
        peak = None
        for c, lo, hi in key_chunks(i):
            s = masked(dot_nt(ke[lo:hi, :], mine), count, start, i, c)
            s_all[lo:hi, view(u)] = s
            top = jnp.max(s, axis=0, keepdims=True)
            peak = top if peak is None else jnp.maximum(peak, top)
        return peak

    def weigh(u, peak):
        i, h = units[u]
        total = 0.0
        for _, lo, hi in key_chunks(i):
            p = jnp.exp(s_all[lo:hi, view(u)] - peak)
            total = total + jnp.sum(p, axis=0, keepdims=True)
            p_all[lo:hi, view(u)] = p.astype(low_type)
        lse[h : h + 1, i * BLOCK : (i + 1) * BLOCK] = peak + jnp.log(total)
        return total

    def collect(u, total):
        i, h = units[u]
        used = PRE + (i + 1) * BLOCK
        feats = slice(h * HEAD, (h + 1) * HEAD)
        o_two[i % 2, feats, :] = dot(vt[feats, 0:used], p_all[0:used, view(u)]) / total
        if h == 1:
            out[i * BLOCK : (i + 1) * BLOCK, :] = o_two[i % 2].T.astype(low_type)

    peak = score(0)
    for u in range(len(units)):
        following = score(u + 1) if u + 1 < len(units) else None
        total = weigh(u, peak)
        collect(u, total)
        peak = following


def attention_backward_pair(
    count, blocks, starts, q, k, v, g, pk, pv, lse, delta, dpk, dpv, ke, ve, kt, p_all, dk, dv
):
    ke[0:PRE, :] = pk[...]
    ke[PRE:, :] = k[...]
    ve[0:PRE, :] = pv[...]
    ve[PRE:, :] = v[...]
    kt[:, 0:PRE] = transposed(pk[...])
    kt[:, PRE:] = transposed(k[...])
    length = blocks * BLOCK

    def weigh(i, h):
        rows = slice(i * BLOCK, (i + 1) * BLOCK)
        mine, grad = head_mask(q[rows, :], h), head_mask(g[rows, :], h)
        start = starts[:, rows]
        shift, middle = lse[h : h + 1, rows], delta[h : h + 1, rows]
        p_at = slice(h * length + i * BLOCK, h * length + (i + 1) * BLOCK)
        ds_at = slice((2 + h) * length + i * BLOCK, (2 + h) * length + (i + 1) * BLOCK)
        for c, lo, hi in key_chunks(i):
            s = masked(dot_nt(ke[lo:hi, :], mine), count, start, i, c)
            p = jnp.exp(s - shift)
            p_all[lo:hi, p_at] = p.astype(low_type)
            ds = p * (dot_nt(ve[lo:hi, :], grad) - middle)
            p_all[lo:hi, ds_at] = ds.astype(low_type)

    def collect_keys(c, h):
        lo, hi, first = (0, PRE, 0) if c < 0 else (PRE + c * BLOCK, PRE + (c + 1) * BLOCK, c * BLOCK)
        mine, grad = head_mask(q[first:length, :], h), head_mask(g[first:length, :], h)
        dv_part = dot(p_all[lo:hi, h * length + first : (h + 1) * length], grad)
        dk_part = dot(p_all[lo:hi, (2 + h) * length + first : (3 + h) * length], mine)
        if h == 0:
            dv[lo:hi, :] = dv_part
            dk[lo:hi, :] = dk_part
        elif c < 0:
            dpv[...] = dv[lo:hi, :] + dv_part
            dpk[...] = dk[lo:hi, :] + dk_part
        else:
            rows = slice(c * BLOCK, (c + 1) * BLOCK)
            v[rows, :] = (dv[lo:hi, :] + dv_part).astype(low_type)
            k[rows, :] = (dk[lo:hi, :] + dk_part).astype(low_type)

    def collect_queries(i, h):
        used = PRE + (i + 1) * BLOCK
        feats = slice(h * HEAD, (h + 1) * HEAD)
        ds_at = slice((2 + h) * length + i * BLOCK, (2 + h) * length + (i + 1) * BLOCK)
        return dot(kt[feats, 0:used], p_all[0:used, ds_at])

    for h in range(2):
        for i in range(blocks):
            weigh(i, h)
    for h in range(2):
        for c in range(-1, blocks):
            collect_keys(c, h)
    for i in range(blocks):
        both = jnp.concatenate([collect_queries(i, 0), collect_queries(i, 1)], 0)
        q[i * BLOCK : (i + 1) * BLOCK, :] = (both.T * (HEAD**-0.5)).astype(low_type)


def block_kernel(
    n,
    n_dp,
    x_hbm,
    starts_hbm,
    cot_hbm,
    w_qkv_hbm,
    w_out_hbm,
    w_fc_hbm,
    w_proj_hbm,
    gain1_ref,
    shift1_ref,
    b_qkv_ref,
    b_out_ref,
    gain2_ref,
    shift2_ref,
    b_fc_ref,
    b_proj_ref,
    table_ref,
    w1_ref,
    b1_ref,
    w2_ref,
    b2_ref,
    out_hbm,
    grad_hbm,
    table_out,
    gw1_out,
    gb1_out,
    gw2_out,
    gb2_out,
    x_rows,
    cot_rows,
    q_s,
    k_s,
    v_s,
    a_s,
    g_s,
    mid,
    h_rows,
    acc_a,
    slope,
    w_qkv,
    w_out,
    w_fc,
    w_proj,
    lse,
    delta,
    ke,
    ve,
    kt,
    dk,
    dv,
    starts_slots,
    starts_row,
    own_pre,
    pre_slots,
    pk_s,
    pv_s,
    hid,
    dp_pre,
    col_slots,
    dp_own,
    dp_own_low,
    dp_slots,
    hid_own,
    hid_slots,
    o_two,
    x_send,
    x_recv,
    s_send,
    s_recv,
    p_send,
    p_recv,
    c_send,
    c_recv,
    o_send,
    o_recv,
    g_send,
    g_recv,
    r_send,
    r_recv,
    d_send,
    d_recv,
    e_send,
    e_recv,
    local_sem,
    fc_sem,
    proj_sem,
    x_here,
    cot_here,
):
    me, me_dp = lax.axis_index("col"), lax.axis_index("dp")
    piece, width = x_hbm.shape[1], x_hbm.shape[2]
    length = n * piece
    blocks = length // BLOCK
    pairs = width // PAIR
    inner = b_fc_ref.shape[0]
    tile = w_fc.shape[2]
    tiles = inner // tile
    rows_pre = table_ref.shape[0]
    group = BLOCK // piece
    part_width = w2_ref.shape[1]
    per_part = part_width // PAIR
    groups = n // group
    heads = 2 * pairs

    def spot(at):
        return pl.ds(pl.multiple_of(at * piece, piece), piece)

    def near(k):
        odd, half = lax.rem(k, 2), lax.div(k + 1, 2)
        return odd * (n - half) + (1 - odd) * half

    def far(m):
        return near(n - 1 - m)

    def each(count, step):
        def body(k, carry):
            step(k)
            return carry

        lax.fori_loop(0, count, body, 0)

    def to(d):
        return lax.rem(me + d, n)

    def source(d):
        return lax.rem(me + n - d, n)

    def remote(src, dst, send, recv, d, axis, peer):
        return pltpu.make_async_remote_copy(
            src_ref=src,
            dst_ref=dst,
            send_sem=send.at[d],
            recv_sem=recv.at[d],
            device_id={axis: peer},
            device_id_type=MESH,
        )

    def vector(ref):
        return ref[...].astype(wide).reshape(1, -1)

    def fc_load(t, slot):
        cols = pl.ds(pl.multiple_of(t * tile, tile), tile)
        return pltpu.make_async_copy(w_fc_hbm.at[:, cols], w_fc.at[slot], fc_sem.at[slot])

    def proj_load(t, slot):
        rows = pl.ds(pl.multiple_of(t * tile, tile), tile)
        return pltpu.make_async_copy(w_proj_hbm.at[rows, :], w_proj.at[slot], proj_sem.at[slot])

    load_qkv = pltpu.make_async_copy(w_qkv_hbm, w_qkv, local_sem.at[0])
    load_qkv.start()
    barrier = pltpu.get_barrier_semaphore()
    for d in range(1, n):
        pl.semaphore_signal(barrier, inc=1, device_id={"col": to(d)}, device_id_type=MESH)
    for d in range(1, n_dp):
        pl.semaphore_signal(
            barrier, inc=1, device_id={"dp": lax.rem(me_dp + d, n_dp)}, device_id_type=MESH
        )
    pl.semaphore_wait(barrier, n - 1 + n_dp - 1)

    def x_copy(d, peer):
        return remote(x_hbm.at[peer], x_rows.at[spot(me), :], x_send, x_recv, d, "col", peer)

    def starts_copy(d, peer):
        return remote(starts_hbm, starts_slots.at[me], s_send, s_recv, d, "col", peer)

    def pre_copy(d, peer):
        return remote(own_pre, pre_slots.at[me], p_send, p_recv, d, "col", peer)

    def cot_copy(d, peer):
        return remote(cot_hbm.at[peer], cot_rows.at[spot(me), :], c_send, c_recv, d, "col", peer)

    def out_copy(d, peer):
        return remote(h_rows.at[spot(peer), :], out_hbm.at[me], o_send, o_recv, d, "col", peer)

    def grad_copy(d, here, peer):
        return remote(here, grad_hbm.at[me], g_send, g_recv, d, "col", peer)

    def send_inputs(m):
        x_copy(far(m), to(far(m))).start()
        starts_copy(far(m), to(far(m))).start()

    each(n - 1, send_inputs)
    own_x = pltpu.make_async_copy(x_hbm.at[me], x_rows.at[spot(me), :], local_sem.at[1])
    own_x.start()
    own_cot = pltpu.make_async_copy(cot_hbm.at[me], cot_rows.at[spot(me), :], local_sem.at[2])
    own_cot.start()
    own_starts = pltpu.make_async_copy(starts_hbm, starts_slots.at[me], local_sem.at[3])
    own_starts.start()
    load_out = pltpu.make_async_copy(w_out_hbm, w_out, local_sem.at[4])
    load_out.start()
    fc_load(0, 0).start()
    proj_load(0, 0).start()

    hidden = jnp.tanh(
        dot(table_ref[...].astype(low_type), w1_ref[...].astype(low_type)) + vector(b1_ref)
    )
    hid[...] = jnp.concatenate([hidden, jnp.zeros((PRE - rows_pre, hidden.shape[1]), wide)], 0)
    own = dot(hidden.astype(low_type), w2_ref[...].astype(low_type)) + vector(b2_ref)
    own = jnp.concatenate([own, jnp.zeros((PRE - rows_pre, part_width), wide)], 0).astype(low_type)
    own_pre[...] = own
    pre_slots[me] = own
    each(n - 1, lambda m: pre_copy(far(m), to(far(m))).start())

    gain1, shift1 = vector(gain1_ref), vector(shift1_ref)
    own_x.wait()
    load_qkv.wait()

    def greet_peers(sem):
        def greet(m):
            pl.semaphore_signal(sem, inc=1, device_id={"col": to(m + 1)}, device_id_type=MESH)

        each(n - 1, greet)

    def qkv_group(g):
        places = []
        for j in range(group):
            k = g * group + j
            d = near(k)
            rows = spot(source(d))
            places.append(rows)

            @pl.when(k > 0)
            def _():
                remote(
                    x_hbm.at[me], x_rows.at[rows, :], x_send, x_recv, d, "col", source(d)
                ).wait_recv()

            normed, _ = standardize(x_rows[rows, :].astype(wide))
            h_rows[j * piece : (j + 1) * piece, :] = (normed * gain1 + shift1).astype(low_type)

        @pl.when(g == groups - 1)
        def _():
            greet_peers(x_here)

        normed = h_rows[0:BLOCK, :]
        for c in range(0, 3 * width, width // 2):
            part = dot(normed, w_qkv[:, c : c + width // 2])
            part = part + b_qkv_ref[c : c + width // 2].astype(wide).reshape(1, -1)
            if c < width:
                part = part * (HEAD**-0.5)
            part = part.astype(low_type)
            slabs = (q_s, k_s, v_s)[c // width]
            for m in range(width // 2 // PAIR):
                pair = (c % width) // PAIR + m
                for j in range(group):
                    slabs[pair, places[j], :] = part[
                        j * piece : (j + 1) * piece, m * PAIR : (m + 1) * PAIR
                    ]

    each(groups, qkv_group)

    pl.semaphore_wait(x_here, n - 1)
    each(n - 1, lambda m: cot_copy(far(m), to(far(m))).start())

    def catch_small(m):
        d = m + 1
        peer = source(d)
        remote(starts_hbm, starts_slots.at[peer], s_send, s_recv, d, "col", peer).wait_recv()
        remote(own_pre, pre_slots.at[peer], p_send, p_recv, d, "col", peer).wait_recv()

    each(n - 1, catch_small)
    own_starts.wait()
    for j in range(n):
        starts_row[:, j * piece : (j + 1) * piece] = starts_slots[j, pl.ds(me, 1), :]
        for m in range(per_part):
            pair = j * per_part + m
            slab = pre_slots[j][:, m * PAIR : (m + 1) * PAIR]
            if pair < pairs:
                pk_s[pair] = slab
            else:
                pv_s[pair - pairs] = slab

    def forward_pair(p):
        attention_forward_pair(
            rows_pre,
            blocks,
            starts_row,
            q_s.at[p],
            k_s.at[p],
            v_s.at[p],
            pk_s.at[p],
            pv_s.at[p],
            a_s.at[p],
            lse.at[p],
            ke,
            kt,
            acc_a,
            slope,
            o_two,
        )

    each(pairs, forward_pair)

    load_out.wait()
    gain2, shift2 = vector(gain2_ref), vector(shift2_ref)
    big = 2 * BLOCK

    def project(b):
        r = pl.ds(pl.multiple_of(b * BLOCK, BLOCK), BLOCK)
        att = jnp.concatenate([a_s[p, r, :] for p in range(pairs)], axis=1)
        middle = x_rows[r, :].astype(wide) + dot(att, w_out[...]) + vector(b_out_ref)
        mid[r, :] = middle
        normed, _ = standardize(middle)
        h_rows[r, :] = (normed * gain2 + shift2).astype(low_type)
        acc_a[r, :] = middle + vector(b_proj_ref)

    each(blocks, project)

    def forward_tile(t):
        slot = lax.rem(t, 2)
        fc_load(t, slot).wait()
        proj_load(t, slot).wait()

        @pl.when(t + 1 < tiles)
        def _():
            fc_load(t + 1, 1 - slot).start()
            proj_load(t + 1, 1 - slot).start()

        cols = pl.ds(pl.multiple_of(t * tile, tile), tile)
        bias = b_fc_ref[cols].astype(wide).reshape(1, -1)

        def half(b):
            r = pl.ds(pl.multiple_of(b * big, big), big)
            upper = dot(h_rows[r, :], w_fc[slot]) + bias
            value, steep = gelu_parts(upper)
            slope[r, cols] = steep.astype(low_type)
            acc_a[r, :] += dot(value.astype(low_type), w_proj[slot])

        each(length // big, half)

    each(tiles, forward_tile)

    def settle(b):
        r = pl.ds(pl.multiple_of(b * BLOCK, BLOCK), BLOCK)
        h_rows[r, :] = acc_a[r, :].astype(low_type)
        acc_a[r, :] = jnp.zeros((BLOCK, width), wide)

    each(blocks, settle)
    own_out = pltpu.make_async_copy(h_rows.at[spot(me), :], out_hbm.at[me], local_sem.at[5])
    own_out.start()
    own_cot.wait()

    def catch_cot(m):
        d = m + 1
        peer = source(d)
        remote(
            cot_hbm.at[me], cot_rows.at[spot(peer), :], c_send, c_recv, d, "col", peer
        ).wait_recv()

    each(n - 1, catch_cot)
    greet_peers(cot_here)

    def backward_tile(step):
        t = tiles - 1 - step
        slot = lax.rem(t, 2)

        @pl.when(step >= 2)
        def _():
            fc_load(t, slot).wait()
            proj_load(t, slot).wait()

        @pl.when(step == 1)
        def _():
            pl.semaphore_wait(cot_here, n - 1)
            each(n - 1, lambda m: out_copy(far(m), to(far(m))).start())

        cols = pl.ds(pl.multiple_of(t * tile, tile), tile)

        def half(b):
            r = pl.ds(pl.multiple_of(b * big, big), big)
            grad_act = dot_nt(cot_rows[r, :], w_proj[slot])
            grad_upper = (grad_act * slope[r, cols].astype(wide)).astype(low_type)
            acc_a[r, :] += dot_nt(grad_upper, w_fc[slot])

        each(length // big, half)

        @pl.when(t >= 2)
        def _():
            fc_load(t - 2, slot).start()
            proj_load(t - 2, slot).start()

    each(tiles, backward_tile)
    feature_head = lax.broadcasted_iota(jnp.int32, (heads, width), 1) // HEAD
    which = lax.broadcasted_iota(jnp.int32, (heads, width), 0)
    member = jnp.where(feature_head == which, 1.0, 0.0).astype(low_type)

    def attend_gradient(b):
        r = pl.ds(pl.multiple_of(b * BLOCK, BLOCK), BLOCK)
        normed, inverse = standardize(mid[r, :])
        grad_mid = cot_rows[r, :].astype(wide) + norm_backward_pass(
            acc_a[r, :], gain2, normed, inverse
        )
        mid[r, :] = grad_mid
        grad_att = dot_nt(grad_mid.astype(low_type), w_out[...]).astype(low_type)
        att = jnp.concatenate([a_s[p, r, :] for p in range(pairs)], axis=1)
        both = grad_att.astype(wide) * att.astype(wide)
        both_low = both.astype(low_type)
        rest = (both - both_low.astype(wide)).astype(low_type)
        sums = dot_nt(member, both_low) + dot_nt(member, rest)
        for p in range(pairs):
            g_s[p, r, :] = grad_att[:, p * PAIR : (p + 1) * PAIR]
            delta[p, :, r] = sums[2 * p : 2 * p + 2, :]

    each(blocks, attend_gradient)

    def backward_pair(p):
        attention_backward_pair(
            rows_pre,
            blocks,
            starts_row,
            q_s.at[p],
            k_s.at[p],
            v_s.at[p],
            g_s.at[p],
            pk_s.at[p],
            pv_s.at[p],
            lse.at[p],
            delta.at[p],
            dp_pre.at[p],
            dp_pre.at[pairs + p],
            ke,
            ve,
            kt,
            slope,
            dk,
            dv,
        )

    each(pairs, backward_pair)

    def part_copy(d, peer):
        mine = dp_pre.at[pl.ds(peer * per_part, per_part)]
        return remote(mine, col_slots.at[me], r_send, r_recv, d, "col", peer)

    def dp_copy(d, peer):
        return remote(dp_own, dp_slots.at[me_dp], d_send, d_recv, d, "dp", peer)

    def hid_copy(d, peer):
        return remote(hid_own, hid_slots.at[me], e_send, e_recv, d, "col", peer)

    each(n - 1, lambda m: part_copy(far(m), to(far(m))).start())
    col_slots[me] = dp_pre[pl.ds(me * per_part, per_part)]

    def sum_slots(slots, count):
        return lax.fori_loop(1, count, lambda j, total: total + slots[j], slots[0])

    def gradient_group(g):
        grads, places = [], []
        for j in range(group):
            rows = spot(to(far(g * group + j)))
            places.append(rows)
            grads.append(
                jnp.concatenate(
                    [slabs[p, rows, :] for slabs in (q_s, k_s, v_s) for p in range(pairs)], axis=1
                )
            )
        back = dot_nt(jnp.concatenate(grads, axis=0), w_qkv[...])
        for j in range(group):
            at = g * group + j
            d = far(at)
            rows = places[j]
            normed, inverse = standardize(x_rows[rows, :].astype(wide))
            total = mid[rows, :] + norm_backward_pass(
                back[j * piece : (j + 1) * piece, :], gain1, normed, inverse
            )
            here = cot_rows.at[spot(at), :]
            here[...] = total.astype(low_type)

            @pl.when(at < n - 1)
            def _():
                grad_copy(d, here, to(d)).start()

            @pl.when(at == n - 1)
            def _():
                pltpu.make_async_copy(here, grad_hbm.at[me], local_sem.at[6]).start()

        @pl.when(g == 0)
        def _():
            def catch_part(m):
                d = m + 1
                peer = source(d)
                mine = dp_pre.at[pl.ds(me * per_part, per_part)]
                remote(mine, col_slots.at[peer], r_send, r_recv, d, "col", peer).wait_recv()

            each(n - 1, catch_part)
            total = sum_slots(col_slots, n)
            total = jnp.concatenate([total[m] for m in range(per_part)], axis=1)
            dp_own[...] = total
            dp_slots[me_dp] = total
            for d in range(1, n_dp):
                dp_copy(d, lax.rem(me_dp + d, n_dp)).start()

        @pl.when(g == 1)
        def _():
            for d in range(1, n_dp):
                peer = lax.rem(me_dp + n_dp - d, n_dp)
                remote(dp_own, dp_slots.at[peer], d_send, d_recv, d, "dp", peer).wait_recv()
            own_grad = sum_slots(dp_slots, n_dp)
            dp_own_low[...] = own_grad.astype(low_type)
            part = dot_nt(dp_own_low[...], w2_ref[...].astype(low_type))
            hid_own[...] = part
            hid_slots[me] = part
            each(n - 1, lambda m: hid_copy(far(m), to(far(m))).start())

    each(groups, gradient_group)
    hidden = hid[...]
    own_low = dp_own_low[...]
    gw2_out[...] = lax.dot_general(
        hidden.astype(low_type), own_low, TN, preferred_element_type=wide
    )
    gb2_out[...] = jnp.sum(own_low.astype(wide), axis=0)

    def catch_hid(m):
        d = m + 1
        peer = source(d)
        remote(hid_own, hid_slots.at[peer], e_send, e_recv, d, "col", peer).wait_recv()

    each(n - 1, catch_hid)
    grad_pre = (sum_slots(hid_slots, n) * (1.0 - hidden * hidden)).astype(low_type)
    table = jnp.concatenate(
        [table_ref[...], jnp.zeros((PRE - rows_pre, table_ref.shape[1]), wide)], 0
    ).astype(low_type)
    gw1_out[...] = lax.dot_general(table, grad_pre, TN, preferred_element_type=wide)
    gb1_out[...] = jnp.sum(grad_pre.astype(wide), axis=0)
    table_out[...] = dot_nt(grad_pre, w1_ref[...].astype(low_type))[:rows_pre, :]

    def finish(m):
        d = m + 1
        peer, here = source(d), cot_rows.at[0:piece, :]
        remote(here, out_hbm.at[peer], o_send, o_recv, d, "col", peer).wait_recv()
        remote(here, grad_hbm.at[peer], g_send, g_recv, d, "col", peer).wait_recv()
        x_copy(d, to(d)).wait_send()
        starts_copy(d, to(d)).wait_send()
        pre_copy(d, to(d)).wait_send()
        cot_copy(d, to(d)).wait_send()
        out_copy(d, to(d)).wait_send()
        grad_copy(d, here, to(d)).wait_send()
        part_copy(d, to(d)).wait_send()
        hid_copy(d, to(d)).wait_send()

    each(n - 1, finish)
    for d in range(1, n_dp):
        dp_copy(d, lax.rem(me_dp + d, n_dp)).wait_send()
    own_out.wait()
    pltpu.make_async_copy(cot_rows.at[0:piece, :], grad_hbm.at[me], local_sem.at[6]).wait()


def on_device(*operands):
    n, n_dp = lax.axis_size("col"), lax.axis_size("dp")
    inputs, starts, cotangent, w_qkv, w_out = [operands[j] for j in (0, 1, 2, 5, 7)]
    w_fc, w_proj, table, w1, w2 = [operands[j] for j in (11, 13, 15, 16, 18)]
    row_count, piece, width = inputs.shape
    assert row_count == n and BLOCK % piece == 0
    length, inner = n * piece, w_fc.shape[1]
    pairs, tile = width // PAIR, min(1024, inner)
    part_width, mid_width = w2.shape[1], w1.shape[1]
    per_part = part_width // PAIR
    ext = PRE + length
    dma = pltpu.SemaphoreType.DMA
    shape = jax.ShapeDtypeStruct
    vmem = pltpu.VMEM
    slabs = vmem((pairs, length, PAIR), low_type)
    ordered = [operands[j] for j in (0, 1, 2, 5, 7, 11, 13)]
    ordered += [operands[j] for j in (3, 4, 6, 8, 9, 10, 12, 14, 15, 16, 17, 18, 19)]
    return tuple(
        pl.pallas_call(
            functools.partial(block_kernel, n, n_dp),
            in_specs=[ANY] * 7 + [VM] * 13,
            out_specs=[ANY, ANY] + [VM] * 5,
            out_shape=[
                shape((n, piece, width), low_type),
                shape((n, piece, width), low_type),
                shape(table.shape, wide),
                shape(w1.shape, wide),
                shape((mid_width,), wide),
                shape(w2.shape, wide),
                shape((part_width,), wide),
            ],
            scratch_shapes=[
                vmem((length, width), low_type),
                vmem((length, width), low_type),
                slabs,
                slabs,
                slabs,
                slabs,
                slabs,
                vmem((length, width), wide),
                vmem((length, width), low_type),
                vmem((ext, width), wide),
                vmem((ext, inner), low_type),
                vmem(w_qkv.shape, low_type),
                vmem(w_out.shape, low_type),
                vmem((2, width, tile), low_type),
                vmem((2, tile, width), low_type),
                vmem((pairs, 2, length), wide),
                vmem((pairs, 2, length), wide),
                vmem((ext, PAIR), low_type),
                vmem((ext, PAIR), low_type),
                vmem((PAIR, ext), low_type),
                vmem((ext, PAIR), wide),
                vmem((ext, PAIR), wide),
                vmem((n,) + starts.shape, jnp.int32),
                vmem((1, length), jnp.int32),
                vmem((PRE, part_width), low_type),
                vmem((n, PRE, part_width), low_type),
                vmem((pairs, PRE, PAIR), low_type),
                vmem((pairs, PRE, PAIR), low_type),
                vmem((PRE, mid_width), wide),
                vmem((2 * pairs, PRE, PAIR), wide),
                vmem((n, per_part, PRE, PAIR), wide),
                vmem((PRE, part_width), wide),
                vmem((PRE, part_width), low_type),
                vmem((n_dp, PRE, part_width), wide),
                vmem((PRE, mid_width), wide),
                vmem((n, PRE, mid_width), wide),
                vmem((2, PAIR, BLOCK), wide),
            ]
            + [dma((n,))] * 14
            + [dma((n_dp,))] * 2
            + [dma((n,))] * 2
            + [dma((7,)), dma((2,)), dma((2,))]
            + [pltpu.SemaphoreType.REGULAR] * 2,
            compiler_params=pltpu.CompilerParams(
                collective_id=0, has_side_effects=True, vmem_limit_bytes=VMEM_BYTES
            ),
        )(*ordered)
    )


def solution(mesh):
    rows = P("dp", "col", None)
    return jax.shard_map(
        on_device,
        mesh=mesh,
        in_specs=(rows, P("dp", "col"), rows) + (P(),) * 15 + (P(None, "col"), P("col")),
        out_specs=(rows, rows, P(), P(), P(), P(None, "col"), P("col")),
        check_vma=False,
    )
```

profile of v0, /device:TPU:0, one launch (start us, length us, event | category | flops | bytes accessed | tf_op | source)
XLA Modules:
  0.0 233.6 jit_solution(13378223720622422830)
XLA Ops:
  0.6 224.8 %shard_map.243 = (bf16[8,128,1024]{2,1,0:T(8,128)(2,1)}, bf16[8,128,1024]{2,1,0:T(8,128)(2,1)}, f32[10,512]{1,0:T(8,128)}, f32[512,512]{1,0:T(8,128)}, f32[512]{...) custom-call(bf16[8,128,1024]{2,1,0:T(8,128)(2,1)} %x_hbm.1, s32[8,128]{1,0:T(8,128)} %starts_hbm.1, ...), custom_call_target="tpu_custom_call" | custom-call | tf_op jit(solution)/shard_map/pallas_call | solution.py:769
  225.5 0.0 copy-start
  225.5 3.2 %copy.34 = bf16[8,128,1024]{2,1,0:T(8,128)(2,1)} copy(bf16[8,128,1024]{2,1,0:T(8,128)(2,1)} %get-tuple-element.14) | data formatting | bytes 4194304
  228.7 0.0 copy-done
  228.7 0.0 copy-start.3
  228.7 0.0 copy-start.1
  228.7 1.3 copy.35
  230.0 0.0 copy-done.3
  230.0 0.0 copy-start.4
  230.0 0.0 copy-start.2
  230.0 0.0 copy-start.5
  230.0 0.6 copy.36
  230.7 0.0 copy-done.1
  230.7 1.0 copy.37
  231.7 0.0 copy-done.4
  231.7 0.6 copy.38
  232.3 0.0 copy-done.2
  232.3 0.8 copy.39
  233.1 0.0 copy-done.5
  233.1 0.6 copy.40
Async XLA Ops:
  225.5 3.2 %copy-start = (bf16[8,128,1024]{2,1,0:T(8,128)(2,1)S(1)}, bf16[8,128,1024]{2,1,0:T(8,128)(2,1)}, u32[]{:S(2)}) copy-start(bf16[8,128,1024]{2,1,0:T(8,128)(2,1)} %get-tuple-element.15) | copy-start | bytes 6291460
  228.7 1.3 copy-start.3
  228.7 2.0 copy-start.1
  230.0 1.6 copy-start.4
  230.0 2.2 copy-start.2
  230.0 3.0 %copy-start.5 = (f32[256]{0:T(256)S(1)}, f32[256]{0:T(256)}, u32[]{:S(2)}) copy-start(f32[256]{0:T(256)} %get-tuple-element.20) | copy-start | bytes 3076
where the time goes:
time: 238 us; the launch traced here: 234 us
  Pallas kernels  225 us (95%)
  local copies, waits for them, and re-layouts  8.14 us (3%)
    pallas_call x1, Pallas kernels, on_device(): pl.pallas_call(functools.partial(block_kernel, n, n_dp), in_specs=[ANY] *...  225 us
    unnamed x19, local copies, waits for them, and re-layouts  8.14 us

commit v1 on v0

--- a/solution.py
+++ b/solution.py
@@ -141,62 +141,125 @@
         peak = following
 
 
-def attention_backward_pair(
-    count, blocks, starts, q, k, v, g, pk, pv, lse, delta, dpk, dpv, ke, ve, kt, p_all, dk, dv
+FINAL, STORE, ADD = range(3)
+
+
+def lower_first_part(blocks):
+    low, high = range(blocks // 2), range(blocks // 2, blocks)
+    work = [(i, range(-1, 0)) for i in low] + [(i, range(-1, i + 1)) for i in high]
+    keys = [(c, range(c, blocks), FINAL) for c in high] + [(c, high, STORE) for c in low]
+    keys += [(-1, range(blocks), FINAL)]
+    return work, keys, [(i, range(-1, i + 1), FINAL) for i in high]
+
+
+def lower_second_part(blocks):
+    low = range(blocks // 2)
+    work = [(i, range(-1, i + 1)) for i in low]
+    keys = [(c, range(c, blocks // 2), ADD) for c in low]
+    return work, keys, [(i, range(-1, i + 1), FINAL) for i in low]
+
+
+def upper_first_part(blocks):
+    half = blocks // 2
+    work = [(i, range(-1, min(i + 1, half))) for i in range(blocks)]
+    keys = [(c, range(max(c, 0), blocks), FINAL) for c in range(-1, half)]
+    queries = [(i, chunks, FINAL if i < half else STORE) for i, chunks in work]
+    return work, keys, queries
+
+
+def upper_second_part(blocks):
+    high = range(blocks // 2, blocks)
+    work = [(i, range(blocks // 2, i + 1)) for i in high]
+    keys = [(c, range(c, blocks), FINAL) for c in high]
+    return work, keys, [(i, chunks, ADD) for i, chunks in work]
+
+
+def key_rows(c):
+    return (0, PRE) if c < 0 else (PRE + c * BLOCK, PRE + (c + 1) * BLOCK)
+
+
+def attention_backward_part(
+    plan, count, starts, q, k, v, g, pk, pv, lse, delta, dpk, dpv, ke, ve, kt, p_all, dk, dv, keep, keep_q
 ):
-    ke[0:PRE, :] = pk[...]
-    ke[PRE:, :] = k[...]
-    ve[0:PRE, :] = pv[...]
-    ve[PRE:, :] = v[...]
-    kt[:, 0:PRE] = transposed(pk[...])
-    kt[:, PRE:] = transposed(k[...])
-    length = blocks * BLOCK
-
-    def weigh(i, h):
+    work, keys, queries = plan
+    length = q.shape[0]
+    half = length // 2
+    used = sorted({c for _, chunks in work for c in chunks})
+    if used[0] < 0:
+        ke[0:PRE, :] = pk[...]
+        ve[0:PRE, :] = pv[...]
+        kt[:, 0:PRE] = transposed(pk[...])
+    first, last = max(used[0], 0) * BLOCK, (used[-1] + 1) * BLOCK
+    ke[PRE + first : PRE + last, :] = k[first:last, :]
+    ve[PRE + first : PRE + last, :] = v[first:last, :]
+    kt[:, PRE + first : PRE + last] = transposed(k[first:last, :])
+
+    def weigh(i, chunks, h):
         rows = slice(i * BLOCK, (i + 1) * BLOCK)
         mine, grad = head_mask(q[rows, :], h), head_mask(g[rows, :], h)
         start = starts[:, rows]
         shift, middle = lse[h : h + 1, rows], delta[h : h + 1, rows]
         p_at = slice(h * length + i * BLOCK, h * length + (i + 1) * BLOCK)
         ds_at = slice((2 + h) * length + i * BLOCK, (2 + h) * length + (i + 1) * BLOCK)
-        for c, lo, hi in key_chunks(i):
+        for c in chunks:
+            lo, hi = key_rows(c)
             s = masked(dot_nt(ke[lo:hi, :], mine), count, start, i, c)
             p = jnp.exp(s - shift)
             p_all[lo:hi, p_at] = p.astype(low_type)
             ds = p * (dot_nt(ve[lo:hi, :], grad) - middle)
             p_all[lo:hi, ds_at] = ds.astype(low_type)
 
-    def collect_keys(c, h):
-        lo, hi, first = (0, PRE, 0) if c < 0 else (PRE + c * BLOCK, PRE + (c + 1) * BLOCK, c * BLOCK)
-        mine, grad = head_mask(q[first:length, :], h), head_mask(g[first:length, :], h)
-        dv_part = dot(p_all[lo:hi, h * length + first : (h + 1) * length], grad)
-        dk_part = dot(p_all[lo:hi, (2 + h) * length + first : (3 + h) * length], mine)
+    def collect_keys(c, members, mode, h):
+        lo, hi = key_rows(c)
+        a, b = members[0] * BLOCK, (members[-1] + 1) * BLOCK
+        mine, grad = head_mask(q[a:b, :], h), head_mask(g[a:b, :], h)
+        dv_part = dot(p_all[lo:hi, h * length + a : h * length + b], grad)
+        dk_part = dot(p_all[lo:hi, (2 + h) * length + a : (2 + h) * length + b], mine)
         if h == 0:
             dv[lo:hi, :] = dv_part
             dk[lo:hi, :] = dk_part
-        elif c < 0:
-            dpv[...] = dv[lo:hi, :] + dv_part
-            dpk[...] = dk[lo:hi, :] + dk_part
-        else:
-            rows = slice(c * BLOCK, (c + 1) * BLOCK)
-            v[rows, :] = (dv[lo:hi, :] + dv_part).astype(low_type)
-            k[rows, :] = (dk[lo:hi, :] + dk_part).astype(low_type)
-
-    def collect_queries(i, h):
-        used = PRE + (i + 1) * BLOCK
-        feats = slice(h * HEAD, (h + 1) * HEAD)
-        ds_at = slice((2 + h) * length + i * BLOCK, (2 + h) * length + (i + 1) * BLOCK)
-        return dot(kt[feats, 0:used], p_all[0:used, ds_at])
+            return
+        dv_part = dv[lo:hi, :] + dv_part
+        dk_part = dk[lo:hi, :] + dk_part
+        if c < 0:
+            dpv[...] = dv_part
+            dpk[...] = dk_part
+            return
+        rows = slice(c * BLOCK, (c + 1) * BLOCK)
+        if mode == STORE:
+            keep[rows, :] = dk_part
+            keep[half + rows.start : half + rows.stop, :] = dv_part
+            return
+        if mode == ADD:
+            dk_part = dk_part + keep[rows, :]
+            dv_part = dv_part + keep[half + rows.start : half + rows.stop, :]
+        v[rows, :] = dv_part.astype(low_type)
+        k[rows, :] = dk_part.astype(low_type)
+
+    def collect_queries(i, chunks, mode):
+        lo, hi = key_rows(chunks[0])[0], key_rows(chunks[-1])[1]
+        parts = []
+        for h in range(2):
+            feats = slice(h * HEAD, (h + 1) * HEAD)
+            ds_at = slice((2 + h) * length + i * BLOCK, (2 + h) * length + (i + 1) * BLOCK)
+            parts.append(dot(kt[feats, lo:hi], p_all[lo:hi, ds_at]))
+        both = jnp.concatenate(parts, 0)
+        kept = slice(i * BLOCK - half, (i + 1) * BLOCK - half)
+        if mode == STORE:
+            keep_q[:, kept] = both
+            return
+        if mode == ADD:
+            both = both + keep_q[:, kept]
+        q[i * BLOCK : (i + 1) * BLOCK, :] = (both.T * (HEAD**-0.5)).astype(low_type)
 
     for h in range(2):
-        for i in range(blocks):
-            weigh(i, h)
+        for i, chunks in work:
+            weigh(i, chunks, h)
     for h in range(2):
-        for c in range(-1, blocks):
-            collect_keys(c, h)
-    for i in range(blocks):
-        both = jnp.concatenate([collect_queries(i, 0), collect_queries(i, 1)], 0)
-        q[i * BLOCK : (i + 1) * BLOCK, :] = (both.T * (HEAD**-0.5)).astype(low_type)
+        for c, members, mode in keys:
+            collect_keys(c, members, mode, h)
+    for i, chunks, mode in queries:
+        collect_queries(i, chunks, mode)
 
 
 def block_kernel(
@@ -261,7 +324,6 @@
     dp_pre,
     col_slots,
     dp_own,
-    dp_own_low,
     dp_slots,
     hid_own,
     hid_slots,
@@ -308,13 +370,6 @@
     def spot(at):
         return pl.ds(pl.multiple_of(at * piece, piece), piece)
 
-    def near(k):
-        odd, half = lax.rem(k, 2), lax.div(k + 1, 2)
-        return odd * (n - half) + (1 - odd) * half
-
-    def far(m):
-        return near(n - 1 - m)
-
     def each(count, step):
         def body(k, carry):
             step(k)
@@ -322,11 +377,22 @@
 
         lax.fori_loop(0, count, body, 0)
 
-    def to(d):
-        return lax.rem(me + d, n)
-
-    def source(d):
-        return lax.rem(me + n - d, n)
+    reach = n // 2
+    mine_base = lax.div(me, reach) * reach
+    other_base = reach - mine_base
+    seat = lax.rem(me, reach)
+
+    def peer_at(m, sign):
+        same = lax.div(m, reach)
+        step = lax.rem(m, reach) + same
+        base = other_base + same * (mine_base - other_base)
+        return base + lax.rem(seat + 2 * reach + sign * step, reach)
+
+    def to(m):
+        return peer_at(m, 1)
+
+    def source(m):
+        return peer_at(m, -1)
 
     def remote(src, dst, send, recv, d, axis, peer):
         return pltpu.make_async_remote_copy(
@@ -352,8 +418,9 @@
     load_qkv = pltpu.make_async_copy(w_qkv_hbm, w_qkv, local_sem.at[0])
     load_qkv.start()
     barrier = pltpu.get_barrier_semaphore()
-    for d in range(1, n):
-        pl.semaphore_signal(barrier, inc=1, device_id={"col": to(d)}, device_id_type=MESH)
+    for m in range(n - 1):
+        peer = to(jnp.int32(m))
+        pl.semaphore_signal(barrier, inc=1, device_id={"col": peer}, device_id_type=MESH)
     for d in range(1, n_dp):
         pl.semaphore_signal(
             barrier, inc=1, device_id={"dp": lax.rem(me_dp + d, n_dp)}, device_id_type=MESH
@@ -379,8 +446,8 @@
         return remote(here, grad_hbm.at[me], g_send, g_recv, d, "col", peer)
 
     def send_inputs(m):
-        x_copy(far(m), to(far(m))).start()
-        starts_copy(far(m), to(far(m))).start()
+        x_copy(m, to(m)).start()
+        starts_copy(m, to(m)).start()
 
     each(n - 1, send_inputs)
     own_x = pltpu.make_async_copy(x_hbm.at[me], x_rows.at[spot(me), :], local_sem.at[1])
@@ -402,7 +469,7 @@
     own = jnp.concatenate([own, jnp.zeros((PRE - rows_pre, part_width), wide)], 0).astype(low_type)
     own_pre[...] = own
     pre_slots[me] = own
-    each(n - 1, lambda m: pre_copy(far(m), to(far(m))).start())
+    each(n - 1, lambda m: pre_copy(m, to(m)).start())
 
     gain1, shift1 = vector(gain1_ref), vector(shift1_ref)
     own_x.wait()
@@ -410,19 +477,18 @@
 
     def greet_peers(sem):
         def greet(m):
-            pl.semaphore_signal(sem, inc=1, device_id={"col": to(m + 1)}, device_id_type=MESH)
+            pl.semaphore_signal(sem, inc=1, device_id={"col": to(m)}, device_id_type=MESH)
 
         each(n - 1, greet)
 
     def qkv_group(g):
         places = []
         for j in range(group):
-            k = g * group + j
-            d = near(k)
+            d = n - 1 - (g * group + j)
             rows = spot(source(d))
             places.append(rows)
 
-            @pl.when(k > 0)
+            @pl.when(d < n - 1)
             def _():
                 remote(
                     x_hbm.at[me], x_rows.at[rows, :], x_send, x_recv, d, "col", source(d)
@@ -453,10 +519,10 @@
     each(groups, qkv_group)
 
     pl.semaphore_wait(x_here, n - 1)
-    each(n - 1, lambda m: cot_copy(far(m), to(far(m))).start())
+    each(n - 1, lambda m: cot_copy(m, to(m)).start())
 
     def catch_small(m):
-        d = m + 1
+        d = m
         peer = source(d)
         remote(starts_hbm, starts_slots.at[peer], s_send, s_recv, d, "col", peer).wait_recv()
         remote(own_pre, pre_slots.at[peer], p_send, p_recv, d, "col", peer).wait_recv()
@@ -544,7 +610,7 @@
     own_cot.wait()
 
     def catch_cot(m):
-        d = m + 1
+        d = m
         peer = source(d)
         remote(
             cot_hbm.at[me], cot_rows.at[spot(peer), :], c_send, c_recv, d, "col", peer
@@ -565,7 +631,7 @@
         @pl.when(step == 1)
         def _():
             pl.semaphore_wait(cot_here, n - 1)
-            each(n - 1, lambda m: out_copy(far(m), to(far(m))).start())
+            each(n - 1, lambda m: out_copy(m, to(m)).start())
 
         cols = pl.ds(pl.multiple_of(t * tile, tile), tile)
 
@@ -606,30 +672,45 @@
 
     each(blocks, attend_gradient)
 
-    def backward_pair(p):
-        attention_backward_pair(
-            rows_pre,
-            blocks,
-            starts_row,
-            q_s.at[p],
-            k_s.at[p],
-            v_s.at[p],
-            g_s.at[p],
-            pk_s.at[p],
-            pv_s.at[p],
-            lse.at[p],
-            delta.at[p],
-            dp_pre.at[p],
-            dp_pre.at[pairs + p],
-            ke,
-            ve,
-            kt,
-            slope,
-            dk,
-            dv,
-        )
-
-    each(pairs, backward_pair)
+    def backward_loop(plan):
+        def backward_pair(p):
+            lanes = pl.ds(pl.multiple_of(p * PAIR, PAIR), PAIR)
+            attention_backward_part(
+                plan,
+                rows_pre,
+                starts_row,
+                q_s.at[p],
+                k_s.at[p],
+                v_s.at[p],
+                g_s.at[p],
+                pk_s.at[p],
+                pv_s.at[p],
+                lse.at[p],
+                delta.at[p],
+                dp_pre.at[p],
+                dp_pre.at[pairs + p],
+                ke,
+                ve,
+                kt,
+                slope,
+                dk,
+                dv,
+                acc_a.at[:, lanes],
+                acc_a.at[lanes, :],
+            )
+
+        each(pairs, backward_pair)
+
+    def backward_by_half(lower, upper):
+        @pl.when(me < reach)
+        def _():
+            backward_loop(lower(blocks))
+
+        @pl.when(me >= reach)
+        def _():
+            backward_loop(upper(blocks))
+
+    backward_by_half(lower_first_part, upper_first_part)
 
     def part_copy(d, peer):
         mine = dp_pre.at[pl.ds(peer * per_part, per_part)]
@@ -641,16 +722,13 @@
     def hid_copy(d, peer):
         return remote(hid_own, hid_slots.at[me], e_send, e_recv, d, "col", peer)
 
-    each(n - 1, lambda m: part_copy(far(m), to(far(m))).start())
-    col_slots[me] = dp_pre[pl.ds(me * per_part, per_part)]
-
     def sum_slots(slots, count):
         return lax.fori_loop(1, count, lambda j, total: total + slots[j], slots[0])
 
     def gradient_group(g):
         grads, places = [], []
         for j in range(group):
-            rows = spot(to(far(g * group + j)))
+            rows = spot(to(g * group + j))
             places.append(rows)
             grads.append(
                 jnp.concatenate(
@@ -660,7 +738,7 @@
         back = dot_nt(jnp.concatenate(grads, axis=0), w_qkv[...])
         for j in range(group):
             at = g * group + j
-            d = far(at)
+            d = at
             rows = places[j]
             normed, inverse = standardize(x_rows[rows, :].astype(wide))
             total = mid[rows, :] + norm_backward_pass(
@@ -677,44 +755,42 @@
             def _():
                 pltpu.make_async_copy(here, grad_hbm.at[me], local_sem.at[6]).start()
 
-        @pl.when(g == 0)
-        def _():
-            def catch_part(m):
-                d = m + 1
-                peer = source(d)
-                mine = dp_pre.at[pl.ds(me * per_part, per_part)]
-                remote(mine, col_slots.at[peer], r_send, r_recv, d, "col", peer).wait_recv()
-
-            each(n - 1, catch_part)
-            total = sum_slots(col_slots, n)
-            total = jnp.concatenate([total[m] for m in range(per_part)], axis=1)
-            dp_own[...] = total
-            dp_slots[me_dp] = total
-            for d in range(1, n_dp):
-                dp_copy(d, lax.rem(me_dp + d, n_dp)).start()
-
-        @pl.when(g == 1)
-        def _():
-            for d in range(1, n_dp):
-                peer = lax.rem(me_dp + n_dp - d, n_dp)
-                remote(dp_own, dp_slots.at[peer], d_send, d_recv, d, "dp", peer).wait_recv()
-            own_grad = sum_slots(dp_slots, n_dp)
-            dp_own_low[...] = own_grad.astype(low_type)
-            part = dot_nt(dp_own_low[...], w2_ref[...].astype(low_type))
-            hid_own[...] = part
-            hid_slots[me] = part
-            each(n - 1, lambda m: hid_copy(far(m), to(far(m))).start())
-
-    each(groups, gradient_group)
+    each(n - 1, lambda m: part_copy(m, to(m)).start())
+    col_slots[me] = dp_pre[pl.ds(me * per_part, per_part)]
+    gradient_group(jnp.int32(0))
+
+    def catch_part(m):
+        peer = source(m)
+        mine = dp_pre.at[pl.ds(me * per_part, per_part)]
+        remote(mine, col_slots.at[peer], r_send, r_recv, m, "col", peer).wait_recv()
+
+    each(n - 1, catch_part)
+    total = sum_slots(col_slots, n)
+    total = jnp.concatenate([total[m] for m in range(per_part)], axis=1)
+    dp_own[...] = total
+    dp_slots[me_dp] = total
+    for d in range(1, n_dp):
+        dp_copy(d, lax.rem(me_dp + d, n_dp)).start()
+    for d in range(1, n_dp):
+        peer = lax.rem(me_dp + n_dp - d, n_dp)
+        remote(dp_own, dp_slots.at[peer], d_send, d_recv, d, "dp", peer).wait_recv()
+    own_low = sum_slots(dp_slots, n_dp).astype(low_type)
+    part = dot_nt(own_low, w2_ref[...].astype(low_type))
+    hid_own[...] = part
+    hid_slots[me] = part
+    each(n - 1, lambda m: hid_copy(m, to(m)).start())
+
+    each(groups // 2 - 1, lambda g: gradient_group(g + 1))
+    backward_by_half(lower_second_part, upper_second_part)
+    each(groups - groups // 2, lambda g: gradient_group(g + groups // 2))
     hidden = hid[...]
-    own_low = dp_own_low[...]
     gw2_out[...] = lax.dot_general(
         hidden.astype(low_type), own_low, TN, preferred_element_type=wide
     )
     gb2_out[...] = jnp.sum(own_low.astype(wide), axis=0)
 
     def catch_hid(m):
-        d = m + 1
+        d = m
         peer = source(d)
         remote(hid_own, hid_slots.at[peer], e_send, e_recv, d, "col", peer).wait_recv()
 
@@ -728,7 +804,7 @@
     table_out[...] = dot_nt(grad_pre, w1_ref[...].astype(low_type))[:rows_pre, :]
 
     def finish(m):
-        d = m + 1
+        d = m
         peer, here = source(d), cot_rows.at[0:piece, :]
         remote(here, out_hbm.at[peer], o_send, o_recv, d, "col", peer).wait_recv()
         remote(here, grad_hbm.at[peer], g_send, g_recv, d, "col", peer).wait_recv()
@@ -746,6 +822,36 @@
         dp_copy(d, lax.rem(me_dp + d, n_dp)).wait_send()
     own_out.wait()
     pltpu.make_async_copy(cot_rows.at[0:piece, :], grad_hbm.at[me], local_sem.at[6]).wait()
+
+
+def hand_over_kernel(count, *refs):
+    given, wanted, held = refs[:count], refs[count : 2 * count], refs[2 * count : 3 * count]
+    sems = refs[3 * count]
+    come = [pltpu.make_async_copy(given[j], held[j], sems.at[0, j]) for j in range(count)]
+    go = [pltpu.make_async_copy(held[j], wanted[j], sems.at[1, j]) for j in range(count)]
+    for copy in come:
+        copy.start()
+    for arrived, copy in zip(come, go):
+        arrived.wait()
+        copy.start()
+    for copy in go:
+        copy.wait()
+
+
+def hand_over(results):
+    results = list(results)
+    count = len(results)
+    return tuple(
+        pl.pallas_call(
+            functools.partial(hand_over_kernel, count),
+            in_specs=[ANY] * count,
+            out_specs=[ANY] * count,
+            out_shape=[jax.ShapeDtypeStruct(r.shape, r.dtype) for r in results],
+            scratch_shapes=[pltpu.VMEM(r.shape, r.dtype) for r in results]
+            + [pltpu.SemaphoreType.DMA((2, count))],
+            compiler_params=pltpu.CompilerParams(vmem_limit_bytes=VMEM_BYTES),
+        )(*results)
+    )
 
 
 def on_device(*operands):
@@ -765,7 +871,7 @@
     slabs = vmem((pairs, length, PAIR), low_type)
     ordered = [operands[j] for j in (0, 1, 2, 5, 7, 11, 13)]
     ordered += [operands[j] for j in (3, 4, 6, 8, 9, 10, 12, 14, 15, 16, 17, 18, 19)]
-    return tuple(
+    return hand_over(
         pl.pallas_call(
             functools.partial(block_kernel, n, n_dp),
             in_specs=[ANY] * 7 + [VM] * 13,
@@ -812,7 +918,6 @@
                 vmem((2 * pairs, PRE, PAIR), wide),
                 vmem((n, per_part, PRE, PAIR), wide),
                 vmem((PRE, part_width), wide),
-                vmem((PRE, part_width), low_type),
                 vmem((n_dp, PRE, part_width), wide),
                 vmem((PRE, mid_width), wide),
                 vmem((n, PRE, mid_width), wide),

time: 238 us -> 228 us (0.958); the launches traced: 234 us -> 228 us
  local copies, waits for them, and re-layouts: 8.14 us -> 0 us
    unnamed x19 -> x0, local copies, waits for them, and re-layouts: 8.14 us -> none
    pallas_call x0 -> x1, Pallas kernels: none -> 4.22 us  [hand_over(): pl.pallas_call(functools.partial(hand_over_kernel, count), in_specs=[ANY]...]
where the time goes in v1:
time: 228 us
  Pallas kernels  227 us (100%)
    pallas_call x1, Pallas kernels, on_device(): pl.pallas_call(functools.partial(block_kernel, n, n_dp), in_specs=[ANY] *...  222 us

profile of v1, /device:TPU:0, one launch (start us, length us, event | category | flops | bytes accessed | tf_op | source)
XLA Modules:
  0.0 227.5 jit_solution(2429278517799277537)
XLA Ops:
  0.6 222.5 %shard_map.243 = (bf16[8,128,1024]{2,1,0:T(8,128)(2,1)}, bf16[8,128,1024]{2,1,0:T(8,128)(2,1)}, f32[10,512]{1,0:T(8,128)}, f32[512,512]{1,0:T(8,128)}, f32[512]{...) custom-call(bf16[8,128,1024]{2,1,0:T(8,128)(2,1)} %x_hbm.1, s32[8,128]{1,0:T(8,128)} %starts_hbm.1, ...), custom_call_target="tpu_custom_call" | custom-call | tf_op jit(solution)/shard_map/pallas_call | solution.py:875
  223.1 4.2 %shard_map.244 = (bf16[8,128,1024]{2,1,0:T(8,128)(2,1)}, bf16[8,128,1024]{2,1,0:T(8,128)(2,1)}, f32[10,512]{1,0:T(8,128)}, f32[512,512]{1,0:T(8,128)}, f32[512]{...) custom-call(bf16[8,128,1024]{2,1,0:T(8,128)(2,1)} %get-tuple-element.14.refs_0_, ...), custom_call_target="tpu_custom_call" | custom-call | tf_op jit(solution)/shard_map/pallas_call | solution.py:845

commit v2 on v1

--- a/solution.py
+++ b/solution.py
@@ -92,23 +92,56 @@
     return values.astype(wide).T.astype(low_type)
 
 
-def attention_forward_pair(count, blocks, starts, q, k, v, pk, pv, out, lse, ke, vt, s_all, p_all, o_two):
-    ke[0:PRE, :] = pk[...]
-    ke[PRE:, :] = k[...]
-    vt[:, 0:PRE] = transposed(pv[...])
-    vt[:, PRE:] = transposed(v[...])
-    units = [(i, h) for i in range(blocks) for h in range(2)]
+FINAL, STORE, ADD = range(3)
+
+
+def own_half_part(blocks, upper):
+    first, last = (blocks // 2, blocks) if upper else (0, blocks // 2)
+    return [(i, range(first, i + 1), STORE) for i in range(first, last)]
+
+
+def other_part(blocks, upper):
+    half = blocks // 2
+    if upper:
+        work = [(i, range(-1, i + 1), FINAL) for i in range(half)]
+        return work + [(i, range(-1, half), ADD) for i in range(half, blocks)]
+    work = [(i, range(-1, 0), ADD) for i in range(half)]
+    return work + [(i, range(-1, i + 1), FINAL) for i in range(half, blocks)]
+
+
+def key_rows(c):
+    return (0, PRE) if c < 0 else (PRE + c * BLOCK, PRE + (c + 1) * BLOCK)
+
+
+def attention_forward_part(
+    work, count, starts, q, k, v, pk, pv, out, lse, ke, vt, s_all, p_all, o_two, keep, keep_stats
+):
+    half = q.shape[0] // 2
+    used = sorted({c for _, chunks, _ in work for c in chunks})
+    if used[0] < 0:
+        ke[0:PRE, :] = pk[...]
+        vt[:, 0:PRE] = transposed(pv[...])
+    first, last = max(used[0], 0) * BLOCK, (used[-1] + 1) * BLOCK
+    if last > first:
+        ke[PRE + first : PRE + last, :] = k[first:last, :]
+        vt[:, PRE + first : PRE + last] = transposed(v[first:last, :])
+    units = [(i, chunks, mode, h) for i, chunks, mode in work for h in range(2)]
 
     def view(u):
         return slice((u % 2) * BLOCK, (u % 2 + 1) * BLOCK)
 
+    def kept(i):
+        first = i * BLOCK % half
+        return slice(first, first + BLOCK)
+
     def score(u):
-        i, h = units[u]
+        i, chunks, mode, h = units[u]
         rows = slice(i * BLOCK, (i + 1) * BLOCK)
         mine = head_mask(q[rows, :], h)
         start = starts[:, rows]
-        peak = None
-        for c, lo, hi in key_chunks(i):
+        peak = keep_stats[h : h + 1, kept(i)] if mode == ADD else None
+        for c in chunks:
+            lo, hi = key_rows(c)
             s = masked(dot_nt(ke[lo:hi, :], mine), count, start, i, c)
             s_all[lo:hi, view(u)] = s
             top = jnp.max(s, axis=0, keepdims=True)
@@ -116,20 +149,31 @@
         return peak
 
     def weigh(u, peak):
-        i, h = units[u]
+        i, chunks, mode, h = units[u]
         total = 0.0
-        for _, lo, hi in key_chunks(i):
+        for c in chunks:
+            lo, hi = key_rows(c)
             p = jnp.exp(s_all[lo:hi, view(u)] - peak)
             total = total + jnp.sum(p, axis=0, keepdims=True)
             p_all[lo:hi, view(u)] = p.astype(low_type)
+        return total
+
+    def collect(u, peak, total):
+        i, chunks, mode, h = units[u]
+        lo, hi = key_rows(chunks[0])[0], key_rows(chunks[-1])[1]
+        feats = slice(h * HEAD, (h + 1) * HEAD)
+        part = dot(vt[feats, lo:hi], p_all[lo:hi, view(u)])
+        if mode == STORE:
+            keep[feats, kept(i)] = part
+            keep_stats[h : h + 1, kept(i)] = peak
+            keep_stats[2 + h : 3 + h, kept(i)] = total
+            return
+        if mode == ADD:
+            shrink = jnp.exp(keep_stats[h : h + 1, kept(i)] - peak)
+            total = total + shrink * keep_stats[2 + h : 3 + h, kept(i)]
+            part = part + shrink * keep[feats, kept(i)]
         lse[h : h + 1, i * BLOCK : (i + 1) * BLOCK] = peak + jnp.log(total)
-        return total
-
-    def collect(u, total):
-        i, h = units[u]
-        used = PRE + (i + 1) * BLOCK
-        feats = slice(h * HEAD, (h + 1) * HEAD)
-        o_two[i % 2, feats, :] = dot(vt[feats, 0:used], p_all[0:used, view(u)]) / total
+        o_two[i % 2, feats, :] = part / total
         if h == 1:
             out[i * BLOCK : (i + 1) * BLOCK, :] = o_two[i % 2].T.astype(low_type)
 
@@ -137,11 +181,8 @@
     for u in range(len(units)):
         following = score(u + 1) if u + 1 < len(units) else None
         total = weigh(u, peak)
-        collect(u, total)
+        collect(u, peak, total)
         peak = following
-
-
-FINAL, STORE, ADD = range(3)
 
 
 def lower_first_part(blocks):
@@ -172,10 +213,6 @@
     work = [(i, range(blocks // 2, i + 1)) for i in high]
     keys = [(c, range(c, blocks), FINAL) for c in high]
     return work, keys, [(i, chunks, ADD) for i, chunks in work]
-
-
-def key_rows(c):
-    return (0, PRE) if c < 0 else (PRE + c * BLOCK, PRE + (c + 1) * BLOCK)
 
 
 def attention_backward_part(
@@ -328,6 +365,7 @@
     hid_own,
     hid_slots,
     o_two,
+    keep_stats,
     x_send,
     x_recv,
     s_send,
@@ -382,17 +420,16 @@
     other_base = reach - mine_base
     seat = lax.rem(me, reach)
 
-    def peer_at(m, sign):
+    def to(m):
         same = lax.div(m, reach)
         step = lax.rem(m, reach) + same
-        base = other_base + same * (mine_base - other_base)
-        return base + lax.rem(seat + 2 * reach + sign * step, reach)
-
-    def to(m):
-        return peer_at(m, 1)
-
-    def source(m):
-        return peer_at(m, -1)
+        there, bit = other_base + same * (mine_base - other_base), 1
+        while bit < reach:
+            differ = lax.rem(lax.div(seat, bit) + lax.div(step, bit), 2)
+            there, bit = there + differ * bit, 2 * bit
+        return there
+
+    source = to
 
     def remote(src, dst, send, recv, d, axis, peer):
         return pltpu.make_async_remote_copy(
@@ -481,10 +518,54 @@
 
         each(n - 1, greet)
 
+    span = n // 2
+    rows_span = span * piece
+
+    def starts_of(first):
+        for j in range(first, first + reach):
+            starts_row[:, j * piece : (j + 1) * piece] = starts_slots[j, pl.ds(me, 1), :]
+
+    def by_half(lower, upper):
+        @pl.when(me < reach)
+        def _():
+            lower()
+
+        @pl.when(me >= reach)
+        def _():
+            upper()
+
+    def forward_loop(work):
+        def forward_pair(p):
+            attention_forward_part(
+                work,
+                rows_pre,
+                starts_row,
+                q_s.at[p],
+                k_s.at[p],
+                v_s.at[p],
+                pk_s.at[p],
+                pv_s.at[p],
+                a_s.at[p],
+                lse.at[p],
+                ke,
+                kt,
+                acc_a,
+                slope,
+                o_two,
+                mid.at[pl.ds(pl.multiple_of(p * PAIR, PAIR), PAIR), :],
+                keep_stats.at[p],
+            )
+
+        each(pairs, forward_pair)
+
+    def catch_starts(m):
+        peer = source(m)
+        remote(starts_hbm, starts_slots.at[peer], s_send, s_recv, m, "col", peer).wait_recv()
+
     def qkv_group(g):
         places = []
-        for j in range(group):
-            d = n - 1 - (g * group + j)
+        for j in range(span):
+            d = n - 1 - (g * span + j)
             rows = spot(source(d))
             places.append(rows)
 
@@ -497,11 +578,11 @@
             normed, _ = standardize(x_rows[rows, :].astype(wide))
             h_rows[j * piece : (j + 1) * piece, :] = (normed * gain1 + shift1).astype(low_type)
 
-        @pl.when(g == groups - 1)
+        @pl.when(g == 1)
         def _():
             greet_peers(x_here)
 
-        normed = h_rows[0:BLOCK, :]
+        normed = h_rows[0:rows_span, :]
         for c in range(0, 3 * width, width // 2):
             part = dot(normed, w_qkv[:, c : c + width // 2])
             part = part + b_qkv_ref[c : c + width // 2].astype(wide).reshape(1, -1)
@@ -511,26 +592,35 @@
             slabs = (q_s, k_s, v_s)[c // width]
             for m in range(width // 2 // PAIR):
                 pair = (c % width) // PAIR + m
-                for j in range(group):
+                for j in range(span):
                     slabs[pair, places[j], :] = part[
                         j * piece : (j + 1) * piece, m * PAIR : (m + 1) * PAIR
                     ]
 
-    each(groups, qkv_group)
+        @pl.when(g == 0)
+        def _():
+            each(reach - 1, lambda m: catch_starts(reach + m))
+            own_starts.wait()
+            by_half(lambda: starts_of(0), lambda: starts_of(reach))
+            by_half(
+                lambda: forward_loop(own_half_part(blocks, False)),
+                lambda: forward_loop(own_half_part(blocks, True)),
+            )
+
+    each(2, qkv_group)
 
     pl.semaphore_wait(x_here, n - 1)
     each(n - 1, lambda m: cot_copy(m, to(m)).start())
 
-    def catch_small(m):
-        d = m
-        peer = source(d)
-        remote(starts_hbm, starts_slots.at[peer], s_send, s_recv, d, "col", peer).wait_recv()
-        remote(own_pre, pre_slots.at[peer], p_send, p_recv, d, "col", peer).wait_recv()
-
-    each(n - 1, catch_small)
-    own_starts.wait()
+    each(reach, catch_starts)
+    by_half(lambda: starts_of(reach), lambda: starts_of(0))
+
+    def catch_prefix(m):
+        peer = source(m)
+        remote(own_pre, pre_slots.at[peer], p_send, p_recv, m, "col", peer).wait_recv()
+
+    each(n - 1, catch_prefix)
     for j in range(n):
-        starts_row[:, j * piece : (j + 1) * piece] = starts_slots[j, pl.ds(me, 1), :]
         for m in range(per_part):
             pair = j * per_part + m
             slab = pre_slots[j][:, m * PAIR : (m + 1) * PAIR]
@@ -539,26 +629,10 @@
             else:
                 pv_s[pair - pairs] = slab
 
-    def forward_pair(p):
-        attention_forward_pair(
-            rows_pre,
-            blocks,
-            starts_row,
-            q_s.at[p],
-            k_s.at[p],
-            v_s.at[p],
-            pk_s.at[p],
-            pv_s.at[p],
-            a_s.at[p],
-            lse.at[p],
-            ke,
-            kt,
-            acc_a,
-            slope,
-            o_two,
-        )
-
-    each(pairs, forward_pair)
+    by_half(
+        lambda: forward_loop(other_part(blocks, False)),
+        lambda: forward_loop(other_part(blocks, True)),
+    )
 
     load_out.wait()
     gain2, shift2 = vector(gain2_ref), vector(shift2_ref)
@@ -599,14 +673,6 @@
 
     each(tiles, forward_tile)
 
-    def settle(b):
-        r = pl.ds(pl.multiple_of(b * BLOCK, BLOCK), BLOCK)
-        h_rows[r, :] = acc_a[r, :].astype(low_type)
-        acc_a[r, :] = jnp.zeros((BLOCK, width), wide)
-
-    each(blocks, settle)
-    own_out = pltpu.make_async_copy(h_rows.at[spot(me), :], out_hbm.at[me], local_sem.at[5])
-    own_out.start()
     own_cot.wait()
 
     def catch_cot(m):
@@ -619,6 +685,17 @@
     each(n - 1, catch_cot)
     greet_peers(cot_here)
 
+    def settle(b):
+        r = pl.ds(pl.multiple_of(b * BLOCK, BLOCK), BLOCK)
+        h_rows[r, :] = acc_a[r, :].astype(low_type)
+        acc_a[r, :] = jnp.zeros((BLOCK, width), wide)
+
+    each(blocks, settle)
+    pl.semaphore_wait(cot_here, n - 1)
+    each(n - 1, lambda m: out_copy(m, to(m)).start())
+    own_out = pltpu.make_async_copy(h_rows.at[spot(me), :], out_hbm.at[me], local_sem.at[5])
+    own_out.start()
+
     def backward_tile(step):
         t = tiles - 1 - step
         slot = lax.rem(t, 2)
@@ -627,11 +704,6 @@
         def _():
             fc_load(t, slot).wait()
             proj_load(t, slot).wait()
-
-        @pl.when(step == 1)
-        def _():
-            pl.semaphore_wait(cot_here, n - 1)
-            each(n - 1, lambda m: out_copy(m, to(m)).start())
 
         cols = pl.ds(pl.multiple_of(t * tile, tile), tile)
 
@@ -702,13 +774,7 @@
         each(pairs, backward_pair)
 
     def backward_by_half(lower, upper):
-        @pl.when(me < reach)
-        def _():
-            backward_loop(lower(blocks))
-
-        @pl.when(me >= reach)
-        def _():
-            backward_loop(upper(blocks))
+        by_half(lambda: backward_loop(lower(blocks)), lambda: backward_loop(upper(blocks)))
 
     backward_by_half(lower_first_part, upper_first_part)
 
@@ -738,26 +804,39 @@
         back = dot_nt(jnp.concatenate(grads, axis=0), w_qkv[...])
         for j in range(group):
             at = g * group + j
-            d = at
             rows = places[j]
             normed, inverse = standardize(x_rows[rows, :].astype(wide))
             total = mid[rows, :] + norm_backward_pass(
                 back[j * piece : (j + 1) * piece, :], gain1, normed, inverse
             )
-            here = cot_rows.at[spot(at), :]
-            here[...] = total.astype(low_type)
-
-            @pl.when(at < n - 1)
-            def _():
-                grad_copy(d, here, to(d)).start()
-
-            @pl.when(at == n - 1)
-            def _():
-                pltpu.make_async_copy(here, grad_hbm.at[me], local_sem.at[6]).start()
+            cot_rows[spot(at), :] = total.astype(low_type)
+
+    def send_gradient(m):
+        here = cot_rows.at[spot(m), :]
+
+        @pl.when(m < n - 1)
+        def _():
+            grad_copy(m, here, to(m)).start()
+
+        @pl.when(m == n - 1)
+        def _():
+            pltpu.make_async_copy(here, grad_hbm.at[me], local_sem.at[6]).start()
+
+    def leave_step(part):
+        def one_group(g):
+            at = part * (groups // 2) + g
+            gradient_group(at)
+            each(group, lambda j: send_gradient(at * group + j))
+
+        each(groups // 2, one_group)
+
+        @pl.when(part == 0)
+        def _():
+            backward_by_half(lower_second_part, upper_second_part)
 
     each(n - 1, lambda m: part_copy(m, to(m)).start())
     col_slots[me] = dp_pre[pl.ds(me * per_part, per_part)]
-    gradient_group(jnp.int32(0))
+    each(2, leave_step)
 
     def catch_part(m):
         peer = source(m)
@@ -780,9 +859,6 @@
     hid_slots[me] = part
     each(n - 1, lambda m: hid_copy(m, to(m)).start())
 
-    each(groups // 2 - 1, lambda g: gradient_group(g + 1))
-    backward_by_half(lower_second_part, upper_second_part)
-    each(groups - groups // 2, lambda g: gradient_group(g + groups // 2))
     hidden = hid[...]
     gw2_out[...] = lax.dot_general(
         hidden.astype(low_type), own_low, TN, preferred_element_type=wide
@@ -790,9 +866,8 @@
     gb2_out[...] = jnp.sum(own_low.astype(wide), axis=0)
 
     def catch_hid(m):
-        d = m
-        peer = source(d)
-        remote(hid_own, hid_slots.at[peer], e_send, e_recv, d, "col", peer).wait_recv()
+        peer = source(m)
+        remote(hid_own, hid_slots.at[peer], e_send, e_recv, m, "col", peer).wait_recv()
 
     each(n - 1, catch_hid)
     grad_pre = (sum_slots(hid_slots, n) * (1.0 - hidden * hidden)).astype(low_type)
@@ -804,24 +879,28 @@
     table_out[...] = dot_nt(grad_pre, w1_ref[...].astype(low_type))[:rows_pre, :]
 
     def finish(m):
-        d = m
-        peer, here = source(d), cot_rows.at[0:piece, :]
-        remote(here, out_hbm.at[peer], o_send, o_recv, d, "col", peer).wait_recv()
-        remote(here, grad_hbm.at[peer], g_send, g_recv, d, "col", peer).wait_recv()
-        x_copy(d, to(d)).wait_send()
-        starts_copy(d, to(d)).wait_send()
-        pre_copy(d, to(d)).wait_send()
-        cot_copy(d, to(d)).wait_send()
-        out_copy(d, to(d)).wait_send()
-        grad_copy(d, here, to(d)).wait_send()
-        part_copy(d, to(d)).wait_send()
-        hid_copy(d, to(d)).wait_send()
+        peer, here = source(m), cot_rows.at[0:piece, :]
+        remote(here, out_hbm.at[peer], o_send, o_recv, m, "col", peer).wait_recv()
+        x_copy(m, to(m)).wait_send()
+        starts_copy(m, to(m)).wait_send()
+        pre_copy(m, to(m)).wait_send()
+        cot_copy(m, to(m)).wait_send()
+        out_copy(m, to(m)).wait_send()
+        part_copy(m, to(m)).wait_send()
+        hid_copy(m, to(m)).wait_send()
 
     each(n - 1, finish)
     for d in range(1, n_dp):
         dp_copy(d, lax.rem(me_dp + d, n_dp)).wait_send()
     own_out.wait()
     pltpu.make_async_copy(cot_rows.at[0:piece, :], grad_hbm.at[me], local_sem.at[6]).wait()
+
+    def finish_gradient(m):
+        peer, here = source(m), cot_rows.at[0:piece, :]
+        remote(here, grad_hbm.at[peer], g_send, g_recv, m, "col", peer).wait_recv()
+        grad_copy(m, here, to(m)).wait_send()
+
+    each(n - 1, finish_gradient)
 
 
 def hand_over_kernel(count, *refs):
@@ -922,6 +1001,7 @@
                 vmem((PRE, mid_width), wide),
                 vmem((n, PRE, mid_width), wide),
                 vmem((2, PAIR, BLOCK), wide),
+                vmem((pairs, 4, length // 2), wide),
             ]
             + [dma((n,))] * 14
             + [dma((n_dp,))] * 2

time: 228 us -> 224 us (0.982)
  Pallas kernels: 227 us -> 223 us
    pallas_call x1, Pallas kernels: 222 us -> 218 us  [on_device(): pl.pallas_call(functools.partial(block_kernel, n, n_dp), in_specs=[ANY] *...]
where the time goes in v2:
time: 224 us; the launch traced here: 223 us
  Pallas kernels  223 us (100%)
    pallas_call x1, Pallas kernels, on_device(): pl.pallas_call(functools.partial(block_kernel, n, n_dp), in_specs=[ANY] *...  218 us

profile of v2, /device:TPU:0, one launch (start us, length us, event | category | flops | bytes accessed | tf_op | source)
XLA Modules:
  0.0 223.4 jit_solution(13987592598123070614)
XLA Ops:
  0.6 218.3 %shard_map.243 = (bf16[8,128,1024]{2,1,0:T(8,128)(2,1)}, bf16[8,128,1024]{2,1,0:T(8,128)(2,1)}, f32[10,512]{1,0:T(8,128)}, f32[512,512]{1,0:T(8,128)}, f32[512]{...) custom-call(bf16[8,128,1024]{2,1,0:T(8,128)(2,1)} %x_hbm.1, s32[8,128]{1,0:T(8,128)} %starts_hbm.1, ...), custom_call_target="tpu_custom_call" | custom-call | tf_op jit(solution)/shard_map/pallas_call | solution.py:954
  219.0 4.2 %shard_map.244 = (bf16[8,128,1024]{2,1,0:T(8,128)(2,1)}, bf16[8,128,1024]{2,1,0:T(8,128)(2,1)}, f32[10,512]{1,0:T(8,128)}, f32[512,512]{1,0:T(8,128)}, f32[512]{...) custom-call(bf16[8,128,1024]{2,1,0:T(8,128)(2,1)} %get-tuple-element.14.refs_0_, ...), custom_call_target="tpu_custom_call" | custom-call | tf_op jit(solution)/shard_map/pallas_call | solution.py:924

commit v3 on v2

--- a/solution.py
+++ b/solution.py
@@ -562,6 +562,10 @@
         peer = source(m)
         remote(starts_hbm, starts_slots.at[peer], s_send, s_recv, m, "col", peer).wait_recv()
 
+    def send_cotangent():
+        pl.semaphore_wait(x_here, n - 1)
+        each(n - 1, lambda m: cot_copy(m, to(m)).start())
+
     def qkv_group(g):
         places = []
         for j in range(span):
@@ -596,6 +600,8 @@
                     slabs[pair, places[j], :] = part[
                         j * piece : (j + 1) * piece, m * PAIR : (m + 1) * PAIR
                     ]
+            if c == width // 2:
+                pl.when(g == 1)(send_cotangent)
 
         @pl.when(g == 0)
         def _():
@@ -609,9 +615,6 @@
 
     each(2, qkv_group)
 
-    pl.semaphore_wait(x_here, n - 1)
-    each(n - 1, lambda m: cot_copy(m, to(m)).start())
-
     each(reach, catch_starts)
     by_half(lambda: starts_of(reach), lambda: starts_of(0))
 
@@ -637,6 +640,14 @@
     load_out.wait()
     gain2, shift2 = vector(gain2_ref), vector(shift2_ref)
     big = 2 * BLOCK
+    halves = [slice(r, r + big) for r in range(0, length, big)]
+
+    def pairwise(step):
+        def two(b):
+            step(2 * b)
+            step(2 * b + 1)
+
+        each(blocks // 2, two)
 
     def project(b):
         r = pl.ds(pl.multiple_of(b * BLOCK, BLOCK), BLOCK)
@@ -647,7 +658,7 @@
         h_rows[r, :] = (normed * gain2 + shift2).astype(low_type)
         acc_a[r, :] = middle + vector(b_proj_ref)
 
-    each(blocks, project)
+    pairwise(project)
 
     def forward_tile(t):
         slot = lax.rem(t, 2)
@@ -662,17 +673,22 @@
         cols = pl.ds(pl.multiple_of(t * tile, tile), tile)
         bias = b_fc_ref[cols].astype(wide).reshape(1, -1)
 
-        def half(b):
-            r = pl.ds(pl.multiple_of(b * big, big), big)
+        for r in halves:
             upper = dot(h_rows[r, :], w_fc[slot]) + bias
             value, steep = gelu_parts(upper)
             slope[r, cols] = steep.astype(low_type)
             acc_a[r, :] += dot(value.astype(low_type), w_proj[slot])
 
-        each(length // big, half)
-
     each(tiles, forward_tile)
 
+    def settle(b):
+        r = pl.ds(pl.multiple_of(b * BLOCK, BLOCK), BLOCK)
+        h_rows[r, :] = acc_a[r, :].astype(low_type)
+        acc_a[r, :] = jnp.zeros((BLOCK, width), wide)
+
+    each(blocks, settle)
+    own_out = pltpu.make_async_copy(h_rows.at[spot(me), :], out_hbm.at[me], local_sem.at[5])
+    own_out.start()
     own_cot.wait()
 
     def catch_cot(m):
@@ -685,16 +701,6 @@
     each(n - 1, catch_cot)
     greet_peers(cot_here)
 
-    def settle(b):
-        r = pl.ds(pl.multiple_of(b * BLOCK, BLOCK), BLOCK)
-        h_rows[r, :] = acc_a[r, :].astype(low_type)
-        acc_a[r, :] = jnp.zeros((BLOCK, width), wide)
-
-    each(blocks, settle)
-    pl.semaphore_wait(cot_here, n - 1)
-    each(n - 1, lambda m: out_copy(m, to(m)).start())
-    own_out = pltpu.make_async_copy(h_rows.at[spot(me), :], out_hbm.at[me], local_sem.at[5])
-    own_out.start()
 
     def backward_tile(step):
         t = tiles - 1 - step
@@ -705,15 +711,16 @@
             fc_load(t, slot).wait()
             proj_load(t, slot).wait()
 
+        @pl.when(step == 1)
+        def _():
+            pl.semaphore_wait(cot_here, n - 1)
+            each(n - 1, lambda m: out_copy(m, to(m)).start())
+
         cols = pl.ds(pl.multiple_of(t * tile, tile), tile)
-
-        def half(b):
-            r = pl.ds(pl.multiple_of(b * big, big), big)
+        for r in halves:
             grad_act = dot_nt(cot_rows[r, :], w_proj[slot])
             grad_upper = (grad_act * slope[r, cols].astype(wide)).astype(low_type)
             acc_a[r, :] += dot_nt(grad_upper, w_fc[slot])
-
-        each(length // big, half)
 
         @pl.when(t >= 2)
         def _():
@@ -742,7 +749,7 @@
             g_s[p, r, :] = grad_att[:, p * PAIR : (p + 1) * PAIR]
             delta[p, :, r] = sums[2 * p : 2 * p + 2, :]
 
-    each(blocks, attend_gradient)
+    pairwise(attend_gradient)
 
     def backward_loop(plan):
         def backward_pair(p):

time: 224 us -> 219 us (0.978)
  Pallas kernels: 223 us -> 218 us
    pallas_call x1, Pallas kernels: 218 us -> 214 us  [on_device(): pl.pallas_call(functools.partial(block_kernel, n, n_dp), in_specs=[ANY] *...]
where the time goes in v3:
time: 219 us
  Pallas kernels  218 us (100%)
    pallas_call x1, Pallas kernels, on_device(): pl.pallas_call(functools.partial(block_kernel, n, n_dp), in_specs=[ANY] *...  214 us

profile of v3, /device:TPU:0, one launch (start us, length us, event | category | flops | bytes accessed | tf_op | source)
XLA Modules:
  0.0 218.9 jit_solution(17311253358119446209)
XLA Ops:
  0.6 213.8 %shard_map.243 = (bf16[8,128,1024]{2,1,0:T(8,128)(2,1)}, bf16[8,128,1024]{2,1,0:T(8,128)(2,1)}, f32[10,512]{1,0:T(8,128)}, f32[512,512]{1,0:T(8,128)}, f32[512]{...) custom-call(bf16[8,128,1024]{2,1,0:T(8,128)(2,1)} %x_hbm.1, s32[8,128]{1,0:T(8,128)} %starts_hbm.1, ...), custom_call_target="tpu_custom_call" | custom-call | tf_op jit(solution)/shard_map/pallas_call | solution.py:961
  214.5 4.2 %shard_map.244 = (bf16[8,128,1024]{2,1,0:T(8,128)(2,1)}, bf16[8,128,1024]{2,1,0:T(8,128)(2,1)}, f32[10,512]{1,0:T(8,128)}, f32[512,512]{1,0:T(8,128)}, f32[512]{...) custom-call(bf16[8,128,1024]{2,1,0:T(8,128)(2,1)} %get-tuple-element.14.refs_0_, ...), custom_call_target="tpu_custom_call" | custom-call | tf_op jit(solution)/shard_map/pallas_call | solution.py:931

commit v4 on v3

--- a/solution.py
+++ b/solution.py
@@ -841,9 +841,10 @@
         def _():
             backward_by_half(lower_second_part, upper_second_part)
 
+    each(2, leave_step)
+
     each(n - 1, lambda m: part_copy(m, to(m)).start())
     col_slots[me] = dp_pre[pl.ds(me * per_part, per_part)]
-    each(2, leave_step)
 
     def catch_part(m):
         peer = source(m)

time: 219 us -> 226 us (1.032)
  Pallas kernels: 218 us -> 225 us
    pallas_call x1, Pallas kernels: 214 us -> 221 us  [on_device(): pl.pallas_call(functools.partial(block_kernel, n, n_dp), in_specs=[ANY] *...]
where the time goes in v4:
time: 226 us
  Pallas kernels  225 us (100%)
    pallas_call x1, Pallas kernels, on_device(): pl.pallas_call(functools.partial(block_kernel, n, n_dp), in_specs=[ANY] *...  221 us

profile of v4, /device:TPU:0, one launch (start us, length us, event | category | flops | bytes accessed | tf_op | source)
XLA Modules:
  0.0 226.3 jit_solution(15079994600966217456)
XLA Ops:
  0.6 221.2 %shard_map.243 = (bf16[8,128,1024]{2,1,0:T(8,128)(2,1)}, bf16[8,128,1024]{2,1,0:T(8,128)(2,1)}, f32[10,512]{1,0:T(8,128)}, f32[512,512]{1,0:T(8,128)}, f32[512]{...) custom-call(bf16[8,128,1024]{2,1,0:T(8,128)(2,1)} %x_hbm.1, s32[8,128]{1,0:T(8,128)} %starts_hbm.1, ...), custom_call_target="tpu_custom_call" | custom-call | tf_op jit(solution)/shard_map/pallas_call | solution.py:962
  221.9 4.2 %shard_map.244 = (bf16[8,128,1024]{2,1,0:T(8,128)(2,1)}, bf16[8,128,1024]{2,1,0:T(8,128)(2,1)}, f32[10,512]{1,0:T(8,128)}, f32[512,512]{1,0:T(8,128)}, f32[512]{...) custom-call(bf16[8,128,1024]{2,1,0:T(8,128)(2,1)} %get-tuple-element.14.refs_0_, ...), custom_call_target="tpu_custom_call" | custom-call | tf_op jit(solution)/shard_map/pallas_call | solution.py:932
